TPU v7x, 32 devices: a whole 2x2x4 slice. The times are simulated.
32 devices in a mesh: groups: 2 (over x), mp: 16 (over z, y, core).
Axes of the slice: x: 2, y: 2, z: 4, core: 2. Of those that a mesh axis runs over, the one named last changes fastest.
Arguments:
- query_grad: bfloat16 [4096, 2048], P(('groups', 'mp')), parts along dimension 0, may hold values from -0.0029296875 to 0.0029296875
- out_basis: bfloat16 [2048, 2048], P('mp'), may hold values from -0.125 to 0.125
- in_basis: bfloat16 [2048, 2048], P('mp'), may hold values from -0.125 to 0.125
- eigen_vals: float32 [2048, 2048], P(None, 'mp'), may hold values from 0.02 to 2
- tok_inputs: bfloat16 [24576, 2048], P('mp'), may hold values from -6 to 6
- tok_grads: bfloat16 [24576, 2048], P('mp'), may hold values from -6 to 6
Outputs:
- scores: float32 [49152], P(('groups', 'mp')), parts along dimension 0
There are 2 independent parts, one for each index of `groups`. A program takes and returns all parts, laid end to end along the dimension named above; an argument that names none is the same for every part. Nothing has to cross between parts.
All inputs are finite; a program needn't handle non-finite values.
Results may differ from a plain program's by a relative error of at most 0.0046.
Values may be sent and summed in bfloat16 or wider, within the bound.
A program may use at most 128 MiB of HBM per device.

v0:
```python
import jax
import jax.numpy as jnp
from jax import lax
from jax.sharding import PartitionSpec as P

damping = 0.05


def shards(query_grad, out_basis, in_basis, eigen_vals, tok_inputs, tok_grads):
    full_in = lax.all_gather(in_basis, "mp", axis=0, tiled=True)
    rotated_in = jnp.dot(query_grad, full_in, preferred_element_type=jnp.float32).astype(
        jnp.bfloat16
    )
    columns = lax.all_to_all(rotated_in, "mp", split_axis=1, concat_axis=0, tiled=True)
    full_out = lax.all_gather(out_basis, "mp", axis=0, tiled=True)
    rotated = lax.dot_general(
        full_out, columns, (((0,), (0,)), ((), ())), preferred_element_type=jnp.float32
    )
    scaled = (rotated / (eigen_vals + damping)).astype(jnp.bfloat16)
    back_out = jnp.dot(full_out, scaled, preferred_element_type=jnp.float32).astype(jnp.bfloat16)
    row_block = lax.all_to_all(back_out, "mp", split_axis=0, concat_axis=1, tiled=True)
    precond = lax.dot_general(
        row_block, full_in, (((1,), (1,)), ((), ())), preferred_element_type=jnp.float32
    ).astype(jnp.bfloat16)
    mapped = lax.dot_general(
        tok_inputs,
        lax.all_gather(precond, "mp", axis=0, tiled=True),
        (((1,), (1,)), ((), ())),
        preferred_element_type=jnp.float32,
    )
    return jnp.sum(tok_grads.astype(jnp.float32) * mapped, axis=1)


def solution(mesh):
    in_specs = (
        P(("groups", "mp"), None),
        P("mp", None),
        P("mp", None),
        P(None, "mp"),
        P("mp", None),
        P("mp", None),
    )
    out_specs = P(("groups", "mp"))
    return jax.shard_map(shards, mesh=mesh, in_specs=in_specs, out_specs=out_specs, check_vma=False)
```

profile of v0, /device:TPU:0, one launch (start us, length us, event | category | flops | bytes accessed | tf_op | source)
XLA Modules:
  0.0 312.2 jit_solution(895775150921105522)
XLA Ops:
  6.5 0.0 copy-start
  6.5 0.0 all-gather.4.cloned.1.call-start
  6.5 0.7 all-gather.4.cloned.1.call-update
  7.3 0.0 all-gather.6.cloned.1.call-start
  7.3 0.7 all-gather.6.cloned.1.call-update
  8.0 0.0 copy-start.1
  8.0 79.1 %all-gather.4.cloned.1.call-done = bf16[2048,2048]{1,0:T(8,128)(2,1)} async-done(((bf16[128,2048]{1,0:T(8,128)(2,1)}), bf16[2048,2048]{1,0:T(8,128)(2,1)}) %all-gather.4.cloned.1.call-update) | async-done | bytes 8388624 | tf_op jit(solution)/shard_map/all_gather | solution.py:10
  87.2 0.0 copy-done
  87.2 4.7 %fusion.3 = bf16[16,16,8,128]{3,2,1,0:T(8,128)(2,1)S(1)} fusion(bf16[128,2048]{1,0:T(8,128)(2,1)S(1)} %copy-done, bf16[2048,2048]{1,0:T(8,128)(2,1)} %all-gather.4.cloned.1.call-done), kind=kOutput, calls=%fused_computation.8 | convolution fusion | flops 1074003968 | bytes 9437184 | tf_op jit(solution)/shard_map/dot_general | solution.py:11
  91.8 0.9 copy.16
  92.8 3.6 %all-to-all-start = ((bf16[128,16,128]{2,0,1:T(8,128)(2,1)}), bf16[128,16,128]{2,0,1:T(8,128)(2,1)S(1)}, u32[]{:S(2)}, u32[]{:S(2)}) async-start(bf16[128,16,128]{2,0,1:T(8,128)(2,1)} %bitcast.37), calls=%async_computation | async-start | bytes 1048576 | tf_op jit(solution)/shard_map/all_to_all | solution.py:14
  96.3 0.0 all-gather.8.cloned.1.call-start
  96.4 77.3 %all-gather.6.cloned.1.call-done = bf16[2048,2048]{1,0:T(8,128)(2,1)} async-done(((bf16[128,2048]{1,0:T(8,128)(2,1)}), bf16[2048,2048]{1,0:T(8,128)(2,1)}) %all-gather.6.cloned.1.call-update) | async-done | bytes 8388624 | tf_op jit(solution)/shard_map/all_gather | solution.py:15
  173.7 0.0 all-to-all-done
  173.7 0.0 copy-done.1
  173.7 14.5 %fusion.4 = bf16[16,16,8,128]{3,2,1,0:T(8,128)(2,1)S(1)} fusion(bf16[2048,2048]{1,0:T(8,128)(2,1)} %all-gather.6.cloned.1.call-done, bf16[2048,128]{1,0:T(8,128)(2,1)S(1)} %bitcast.40, f32[2048,128]{1,0:T(8,128)S(1)} %copy-done.1), kind=kOutput, calls=%fused_computation.9 | convolution fusion | flops 2148532224 | bytes 10485760 | tf_op jit(solution)/shard_map/dot_general | solution.py:20
  188.1 0.1 copy.15
  188.3 17.3 %all_to_all.38 = bf16[16,128,128]{1,2,0:T(8,128)(2,1)S(1)} all-to-all(bf16[16,128,128]{1,2,0:T(8,128)(2,1)S(1)} %bitcast.39), channel_id=1, replica_groups=mesh['groups'=2,'mp'=16] {'mp'}, dimensions={0} | all-to-all | bytes 1048576 | tf_op jit(solution)/shard_map/all_to_all | solution.py:21
  205.6 7.1 %convolution_convert_fusion = bf16[128,2048]{1,0:T(8,128)(2,1)} fusion(bf16[128,2048]{0,1:T(8,128)(2,1)S(1)} %bitcast.38, bf16[2048,2048]{1,0:T(8,128)(2,1)} %all-gather.4.cloned.1.call-done), kind=kOutput, calls=%fused_computation.3 | convolution fusion | flops 1074003968 | bytes 9437184 | tf_op jit(solution)/shard_map/dot_general | solution.py:22
  212.7 0.0 all-gather.8.cloned.1.call-update
  212.7 8.6 %copy.8 = bf16[1536,2048]{0,1:T(8,128)(2,1)} copy(bf16[1536,2048]{1,0:T(8,128)(2,1)} %param.11) | data formatting | bytes 12582912 | tf_op args[5]
  221.4 65.7 %all-gather.8.cloned.1.call-done = bf16[2048,2048]{1,0:T(8,128)(2,1)} async-done(((bf16[128,2048]{1,0:T(8,128)(2,1)}), bf16[2048,2048]{1,0:T(8,128)(2,1)}) %all-gather.8.cloned.1.call-update) | async-done | bytes 8388624 | tf_op jit(solution)/shard_map/all_gather | solution.py:27
  287.1 18.6 %fusion = f32[1536]{0:T(1024)} fusion(bf16[1536,2048]{0,1:T(8,128)(2,1)} %copy.8, bf16[2048,2048]{1,0:T(8,128)(2,1)} %all-gather.8.cloned.1.call-done, bf16[1536,2048]{1,0:T(8,128)(2,1)} %param.10), kind=kOutput, calls=%fused_computation.1 | convolution fusion | flops 12894337024 | bytes 20977664 | tf_op jit(solution)/shard_map/dot_general | solution.py:25
Async XLA Ops:
  6.5 80.6 %copy-start = (bf16[128,2048]{1,0:T(8,128)(2,1)S(1)}, bf16[128,2048]{1,0:T(8,128)(2,1)}, u32[]{:S(2)}) copy-start(bf16[128,2048]{1,0:T(8,128)(2,1)} %param.6) | copy-start | bytes 1572868
  6.5 80.6 %all-gather.4.cloned.1.call-start = ((), (), s32[]{:S(2)}) async-start(), calls=%async_computation.2 | async-start | bytes 8912896 | tf_op jit(solution)/shard_map/all_gather | solution.py:10
  7.3 166.4 %all-gather.6.cloned.1.call-start = ((), (), s32[]{:S(2)}) async-start(), calls=%async_computation.3 | async-start | bytes 8912896 | tf_op jit(solution)/shard_map/all_gather | solution.py:15
  8.0 165.7 %copy-start.1 = (f32[2048,128]{1,0:T(8,128)S(1)}, f32[2048,128]{1,0:T(8,128)}, u32[]{:S(2)}) copy-start(f32[2048,128]{1,0:T(8,128)} %param.9) | copy-start | bytes 3145732
  92.8 80.9 %all-to-all-start = ((bf16[128,16,128]{2,0,1:T(8,128)(2,1)}), bf16[128,16,128]{2,0,1:T(8,128)(2,1)S(1)}, u32[]{:S(2)}, u32[]{:S(2)}) async-start(bf16[128,16,128]{2,0,1:T(8,128)(2,1)} %bitcast.37), calls=%async_computation | async-start | bytes 1048576 | tf_op jit(solution)/shard_map/all_to_all | solution.py:14
  96.3 190.7 %all-gather.8.cloned.1.call-start = ((), (), s32[]{:S(2)}) async-start(), calls=%async_computation.4 | async-start | bytes 8912896 | tf_op jit(solution)/shard_map/all_gather | solution.py:27
Sparse Core Ops, SparseCore 0:
  9.5 77.5 all-gather.3
  89.3 84.2 all-gather.5
  212.8 74.2 all-gather.7
where the time goes:
time: 313 us; the launch traced here: 312 us
  waiting for transfers between devices  224 us (72%)
  matrix products  44.9 us (14%)
  blocking collectives  17.3 us (6%)
  between operations  13.1 us (4%)
  local copies, waits for them, and re-layouts  9.72 us (3%)
  starting transfers between devices  3.66 us (1%)
    all_gather x1, waiting for transfers between devices, shards(): full_in = lax.all_gather(in_basis, 'mp', axis=0, tiled=True)  79.1 us
    all_gather x1, waiting for transfers between devices, shards(): full_out = lax.all_gather(out_basis, 'mp', axis=0, tiled=True)  77.3 us
    all_gather x1, waiting for transfers between devices, shards(): lax.all_gather(precond, 'mp', axis=0, tiled=True)  65.7 us
    dot_general x1, matrix products, shards(): lax.dot_general(tok_inputs, lax.all_gather(precond, 'mp', axis=0, tiled=T...  18.6 us
    all_to_all x1, blocking collectives, shards(): lax.all_to_all(back_out, 'mp', split_axis=0, concat_axis=1, tiled=True)  17.3 us
    dot_general x1, matrix products, shards(): jnp.dot(full_out, scaled, preferred_element_type=jnp.float32)  14.5 us
    unnamed x5, local copies, waits for them, and re-layouts  8.65 us
    dot_general x1, matrix products, shards(): lax.dot_general(row_block, full_in, (((1,), (1,)), ((), ())), preferred_e...  7.12 us
  transfers between devices with their start and end apart: 4, of which 3 were waited for; matrix products, arithmetic and copies ran while one was open for 5% of the time, Pallas kernels for 0%

commit v1 on v0

v1 whole, which is shorter than its diff:
```python
import functools

import jax
import jax.numpy as jnp
from jax import lax
from jax.experimental import pallas as pl
from jax.experimental.pallas import tpu as pltpu
from jax.sharding import PartitionSpec as P

damping = 0.05
BF, F32 = jnp.bfloat16, jnp.float32
MESH = pl.DeviceIdType.MESH


class Place:
    def __init__(self, n, groups):
        self.n, self.nz = n, n // 4
        self.me = lax.axis_index("mp")
        self.g = lax.axis_index("groups")
        self.par = lax.rem(self.g, 2)
        self.c = lax.rem(self.me, 2)
        self.y = lax.rem(self.me // 2, 2)
        self.z = self.me // 4
        self.xdev = {"groups": self.g + 1 - 2 * self.par}
        self.ydev = {"mp": self.me + 2 - 4 * self.y}
        self.cdev = {"mp": self.me + 1 - 2 * self.c}

    def block(self, z, rel_y, rel_c=0):
        y = self.y if rel_y == 0 else 1 - self.y
        c = self.c if rel_c == 0 else 1 - self.c
        return (z * 2 + y) * 2 + c


class Gather:
    def __init__(self, place, buf, rows, send, recv, share):
        self.p, self.buf, self.rows, self.send, self.recv = place, buf, rows, send, recv
        self.share = share
        self.h = (rows * 3 // 8 + 15) // 16 * 16 if share else 0

    def part(self, kind, block):
        rows, h, p = self.rows, self.h, self.p
        if kind == "all":
            start, size = block * rows, rows
        elif kind == "carried":
            start, size = block * rows + (p.par * h if h else 0), rows - h
        elif kind == "mine":
            start, size = block * rows + p.par * (rows - h), h
        else:
            start, size = block * rows + (1 - p.par) * (rows - h), h
        return self.buf.at[pl.ds(pl.multiple_of(start, 16), size), :]

    def copy(self, ref, kind, sd, rd, dev):
        return pltpu.make_async_remote_copy(
            src_ref=ref,
            dst_ref=ref,
            send_sem=self.send.at[kind, sd],
            recv_sem=self.recv.at[kind, rd],
            device_id=dev,
            device_id_type=MESH,
        )

    def sem(self, d, s):
        return d * self.p.nz + s

    def copies(self, what, d, s):
        p = self.p
        zs = p.z + s if d == 0 else p.z - s
        i = self.sem(d, s)
        if what == "z":
            nxt = p.me - 4 if d == 0 else p.me + 4
            return self.copy(
                self.part("carried", p.block(zs, 0)), 0, i, self.sem(d, s + 1), {"mp": nxt}
            )
        if what == "y":
            return self.copy(self.part("carried", p.block(zs, 0)), 1, i, i, p.ydev)
        kind, rel = what
        if kind == "x":
            return self.copy(self.part("mine", p.block(zs, rel)), 2 + rel, i, i, p.xdev)
        return self.copy(self.part("all", p.block(zs, rel)), 4 + rel, i, i, p.cdev)

    def arrived(self, what, d, s):
        p = self.p
        zs = p.z + s if d == 0 else p.z - s
        i = self.sem(d, s)
        if what == "z":
            self.copy(self.part("carried", p.block(zs, 0)), 0, i, i, p.ydev).wait_recv()
        elif what == "y":
            self.copy(self.part("carried", p.block(zs, 1)), 1, i, i, p.ydev).wait_recv()
        else:
            kind, rel = what
            if kind == "x":
                self.copy(self.part("other", p.block(zs, rel)), 2 + rel, i, i, p.xdev).wait_recv()
            else:
                ref = self.part("all", p.block(zs, rel, 1))
                self.copy(ref, 4 + rel, i, i, p.cdev).wait_recv()

    def there(self, d, s):
        return self.p.z + s < self.p.nz if d == 0 else self.p.z - s >= 0

    def onward(self, d):
        return self.p.z > 0 if d == 0 else self.p.z < self.p.nz - 1

    def each(self, s, f):
        if s == 0:
            f(0, 0)
            return
        for d in (0, 1):
            pl.when(self.there(d, s))(functools.partial(f, d, s))

    def begin(self):
        for d in (0, 1):
            pl.when(self.onward(d))(lambda d=d: self.copies("z", d, 0).start())
        self.copies("y", 0, 0).start()
        self.copies(("c", 0), 0, 0).start()

    def z_step(self, s):
        def f(d, s):
            self.arrived("z", d, s)
            if s < self.p.nz - 1:
                pl.when(self.onward(d))(lambda: self.copies("z", d, s).start())
            self.copies("y", d, s).start()
            if self.share:
                self.copies(("x", 0), d, s).start()
            else:
                self.copies(("c", 0), d, s).start()

        self.each(s, f)

    def y_step(self, s):
        def f(d, s):
            self.arrived("y", d, s)
            self.copies(("x", 1) if self.share else ("c", 1), d, s).start()

        self.each(s, f)

    def x_step(self, s):
        if not self.share:
            return

        def f(d, s):
            if s > 0:
                self.arrived(("x", 0), d, s)
                self.copies(("c", 0), d, s).start()
            self.arrived(("x", 1), d, s)
            self.copies(("c", 1), d, s).start()

        self.each(s, f)

    def c_step(self, s):
        def f(d, s):
            self.arrived(("c", 0), d, s)
            self.arrived(("c", 1), d, s)

        self.each(s, f)

    def end(self):
        for s in range(self.p.nz):

            def f(d, s):
                self.copies("y", d, s).wait_send()
                self.copies(("c", 0), d, s).wait_send()
                self.copies(("c", 1), d, s).wait_send()
                if self.share:
                    if s > 0:
                        self.copies(("x", 0), d, s).wait_send()
                    self.copies(("x", 1), d, s).wait_send()
                if 0 < s < self.p.nz - 1:
                    pl.when(self.onward(d))(lambda: self.copies("z", d, s).wait_send())

            self.each(s, f)
        for d in (0, 1):
            pl.when(self.onward(d))(lambda d=d: self.copies("z", d, 0).wait_send())


def tiles(width, f, size=512):
    @pl.loop(0, width // size)
    def _(i):
        f(pl.ds(pl.multiple_of(i * size, size), size))


def kernel(
    n, groups, q_in, uo_in, ui_in, eig_in, tok_in, grad_in, out,
    ui, uo, bt, tok, tin, acc, q, eig, m1t, xs, st,
    isend, irecv, osend, orecv, bsend, brecv, asend, arecv, local,
):
    p = Place(n, groups)
    nz, me = p.nz, p.me
    rows, width = q.shape
    do = uo.shape[1]
    tokens = tok.shape[0]
    own = pl.ds(pl.multiple_of(me * rows, rows), rows)

    loads = [
        pltpu.make_async_copy(src, dst, local.at[k])
        for k, (src, dst) in enumerate(
            [(ui_in, ui.at[own, :]), (uo_in, uo.at[own, :]), (q_in, q), (tok_in, tok), (eig_in, eig)]
        )
    ]
    for load in loads:
        load.start()

    barrier = pltpu.get_barrier_semaphore()
    for k in range(1, n):
        pl.semaphore_signal(barrier, inc=1, device_id={"mp": lax.rem(me + k, n)}, device_id_type=MESH)
    pl.semaphore_signal(barrier, inc=1, device_id=p.xdev, device_id_type=MESH)
    pl.semaphore_wait(barrier, n)

    gi = Gather(p, ui, rows, isend, irecv, True)
    go = Gather(p, uo, rows, osend, orecv, True)
    gb = Gather(p, bt, rows, bsend, brecv, False)

    loads[0].wait()
    gi.begin()
    for s in range(1, nz):
        gi.z_step(s)
        gi.y_step(s - 1)
        if s >= 2:
            gi.x_step(s - 2)
    gi.y_step(nz - 1)
    loads[1].wait()
    go.begin()
    gi.x_step(nz - 2)
    gi.x_step(nz - 1)
    for s in range(nz):
        gi.c_step(s)

    loads[2].wait()

    def first(cols):
        m1 = jnp.dot(q[...], ui[:, cols], preferred_element_type=F32)
        m1t[cols, :] = m1.T.astype(BF)

    tiles(width, first)
    xs[pl.ds(me, 1)] = m1t[own, :][None]

    def exchange(k):
        to = lax.rem(me + k, n)
        return pltpu.make_async_remote_copy(
            src_ref=m1t.at[pl.ds(pl.multiple_of(to * rows, rows), rows), :],
            dst_ref=xs.at[me],
            send_sem=asend.at[k],
            recv_sem=arecv.at[k],
            device_id={"mp": to},
            device_id_type=MESH,
        )

    def exchanged(k):
        return pltpu.make_async_remote_copy(
            src_ref=m1t.at[own, :],
            dst_ref=xs.at[lax.rem(me + n - k, n)],
            send_sem=asend.at[k],
            recv_sem=arecv.at[k],
            device_id={"mp": lax.rem(me + k, n)},
            device_id_type=MESH,
        )

    for k in range(1, n):
        exchange(k).start()

    loads[3].wait()
    piece = tokens // nz

    def rotate_tokens(s):
        r = pl.ds(s * piece, piece)

        def f(cols):
            tin[r, cols] = jnp.dot(tok[r, :], ui[:, cols], preferred_element_type=F32).astype(BF)

        tiles(width, f)

    for s in range(1, nz):
        go.z_step(s)
        go.y_step(s - 1)
        if s >= 2:
            go.x_step(s - 2)
        rotate_tokens(s - 1)
    go.y_step(nz - 1)
    go.x_step(nz - 2)
    rotate_tokens(nz - 1)
    grads = pltpu.make_async_copy(grad_in, tok, local.at[5])
    grads.start()
    go.x_step(nz - 1)
    for s in range(nz):
        go.c_step(s)
    for k in range(1, n):
        exchanged(k).wait_recv()
    loads[4].wait()

    def second(cols):
        if rows % 128 == 0:
            left = jnp.concatenate([xs[j] for j in range(n)], axis=1)
            r = jnp.dot(left, uo[:, cols], preferred_element_type=F32)
        else:
            r = jnp.zeros((rows, 512), F32)
            for j in range(n):
                r += jnp.dot(
                    xs[j], uo[pl.ds(j * rows, rows), cols], preferred_element_type=F32
                )
        st[:, cols] = (r / (eig[cols, :].T + damping)).astype(BF)

    tiles(do, second)

    def third(cols):
        b = lax.dot_general(
            st[...], uo[cols, :], (((1,), (1,)), ((), ())), preferred_element_type=F32
        )
        bt[own, cols] = b.astype(BF)

    tiles(do, third)
    gb.begin()

    step = 384 if tokens % 384 == 0 else tokens

    def add_plane(first, d, s):
        zs = p.z + s if d == 0 else p.z - s
        k = pl.ds(pl.multiple_of(zs * 4 * rows, 4 * rows), 4 * rows)

        @pl.loop(0, tokens // step)
        def _(t):
            r = pl.ds(pl.multiple_of(t * step, step), step)

            def f(cols):
                new = jnp.dot(tin_part(r, zs), bt[k, cols], preferred_element_type=F32)
                if first:
                    acc[r, cols] = new
                else:
                    acc[r, cols] += new

            tiles(do, f)

    def tin_part(r, zs):
        if 4 * rows % 128 == 0:
            return tin[r, pl.ds(pl.multiple_of(zs * 4 * rows, 4 * rows), 4 * rows)]
        raise ValueError("rows")

    for s in range(1, nz):
        gb.z_step(s)
        gb.y_step(s - 1)
        gb.c_step(s - 1)
        if s == 1:
            add_plane(True, 0, 0)
        else:
            gb.each(s - 1, functools.partial(add_plane, False))
    gb.y_step(nz - 1)
    gb.c_step(nz - 1)
    gb.each(nz - 1, functools.partial(add_plane, False))

    grads.wait()
    step2 = out.shape[1]

    @pl.loop(0, out.shape[0])
    def _(t):
        r = pl.ds(pl.multiple_of(t * step2, step2), step2)
        part = jnp.zeros((step2, 128), F32)
        for j in range(do // 128):
            cols = slice(j * 128, (j + 1) * 128)
            part += tok[r, cols].astype(F32) * acc[r, cols]
        out[pl.ds(t, 1), :] = jnp.sum(part.T, axis=0, keepdims=True)

    for g in (gi, go, gb):
        g.end()
    for k in range(1, n):
        exchange(k).wait_send()


def solution(mesh):
    n, groups = mesh.shape["mp"], mesh.shape["groups"]

    def shards(query_grad, out_basis, in_basis, eigen_vals, tok_inputs, tok_grads):
        rows, di = query_grad.shape
        do = out_basis.shape[1]
        tokens = tok_inputs.shape[0]
        nz = n // 4
        dma = pltpu.SemaphoreType.DMA
        scores = pl.pallas_call(
            functools.partial(kernel, n, groups),
            out_shape=jax.ShapeDtypeStruct((tokens // 128, 128), F32),
            in_specs=[pl.BlockSpec(memory_space=pl.ANY)] * 6,
            out_specs=pl.BlockSpec(memory_space=pltpu.VMEM),
            scratch_shapes=[
                pltpu.VMEM((di, di), BF),
                pltpu.VMEM((do, do), BF),
                pltpu.VMEM((di, do), BF),
                pltpu.VMEM((tokens, di), BF),
                pltpu.VMEM((tokens, di), BF),
                pltpu.VMEM((tokens, do), F32),
                pltpu.VMEM((rows, di), BF),
                pltpu.VMEM((do, eigen_vals.shape[1]), F32),
                pltpu.VMEM((di, rows), BF),
                pltpu.VMEM((n, rows, rows), BF),
                pltpu.VMEM((rows, do), BF),
            ]
            + [dma((6, 2 * nz))] * 6
            + [dma((n,)), dma((n,)), dma((6,))],
            compiler_params=pltpu.CompilerParams(
                collective_id=0, has_side_effects=True, vmem_limit_bytes=60 * 2**20
            ),
        )(query_grad, out_basis, in_basis, eigen_vals, tok_inputs, tok_grads)
        return scores.reshape(tokens)

    in_specs = (
        P(("groups", "mp"), None),
        P("mp", None),
        P("mp", None),
        P(None, "mp"),
        P("mp", None),
        P("mp", None),
    )
    out_specs = P(("groups", "mp"))
    return jax.shard_map(shards, mesh=mesh, in_specs=in_specs, out_specs=out_specs, check_vma=False)
```

time: 313 us -> 165 us (0.53)
  waiting for transfers between devices: 224 us -> 0 us
  Pallas kernels: 0 us -> 162 us
  matrix products: 44.9 us -> 0 us
  blocking collectives: 17.3 us -> 0 us
  between operations: 13.1 us -> 0.01 us
  local copies, waits for them, and re-layouts: 9.72 us -> 1.3 us
  starting transfers between devices: 3.66 us -> 0 us
    all_gather x3 -> x0, waiting for transfers between devices: 222 us -> none  [the longest x1 79.1 us: shards(): full_in = lax.all_gather(in_basis, 'mp', axis=0, tiled=True)]
    pallas_call x0 -> x1, Pallas kernels: none -> 162 us  [shards(): pl.pallas_call(functools.partial(kernel, n, groups), out_shape=jax.ShapeD...]
    dot_general x4 -> x0, matrix products: 44.9 us -> none  [the longest x1 18.6 us: shards(): lax.dot_general(tok_inputs, lax.all_gather(precond, 'mp', axis=0, tiled=T...]
    all_to_all x1 -> x0, blocking collectives: 17.3 us -> none  [shards(): lax.all_to_all(back_out, 'mp', split_axis=0, concat_axis=1, tiled=True)]
    unnamed x5 -> x1, local copies, waits for them, and re-layouts: 8.65 us -> 1.3 us
    all_to_all x1 -> x0, starting transfers between devices: 3.57 us -> none  [shards(): lax.all_to_all(rotated_in, 'mp', split_axis=1, concat_axis=0, tiled=True)]
  transfers between devices with their start and end apart: 4 -> 0, of which waited for: 3 -> 0; matrix products, arithmetic and copies ran while one was open for 5% -> 0% of each run, Pallas kernels for 0% -> 0%
where the time goes in v1:
time: 165 us; the launch traced here: 163 us
  Pallas kernels  162 us (98%)
    pallas_call x1, Pallas kernels, shards(): pl.pallas_call(functools.partial(kernel, n, groups), out_shape=jax.ShapeD...  162 us

profile of v1, /device:TPU:0, one launch (start us, length us, event | category | flops | bytes accessed | tf_op | source)
XLA Modules:
  0.0 162.9 jit_solution(1810395907529250839)
XLA Ops:
  0.0 161.6 %shard_map.64 = f32[12,128]{1,0:T(8,128)} custom-call(bf16[128,2048]{1,0:T(8,128)(2,1)} %q_in.1, bf16[128,2048]{1,0:T(8,128)(2,1)} %uo_in.1, bf16[128,2048]{1,0:T(8,128)(2,1)} %ui_in.1, f32[2048,128]{1,0:T(8,128)} %eig_in.1, bf16[1536,2048]{1,0:T(8,128)(2,1)} %tok_in.1, bf16[1536,2048]{1,0:T(8,128)(2,1)} %grad_in.1), custom_call_target="tpu_custom_call" | custom-call | tf_op jit(solution)/shard_map/pallas_call | solution.py:375
  161.6 1.3 copy.8

commit v2 on v1

--- a/solution.py
+++ b/solution.py
@@ -10,6 +10,7 @@
 damping = 0.05
 BF, F32 = jnp.bfloat16, jnp.float32
 MESH = pl.DeviceIdType.MESH
+CHUNKS = 2
 
 
 class Place:
@@ -32,24 +33,33 @@
 
 
 class Gather:
-    def __init__(self, place, buf, rows, send, recv, share):
+    def __init__(self, place, buf, rows, send, recv, share, chunk):
         self.p, self.buf, self.rows, self.send, self.recv = place, buf, rows, send, recv
+        self.chunk = chunk
+        self.width = buf.shape[1] // CHUNKS
+        self.cols = pl.ds(chunk * self.width, self.width)
         self.share = share
         self.h = (rows * 3 // 8 + 15) // 16 * 16 if share else 0
+        self.dup = 0
 
     def part(self, kind, block):
         rows, h, p = self.rows, self.h, self.p
         if kind == "all":
             start, size = block * rows, rows
+        elif kind == "dup":
+            start, size = block * rows, self.dup
+        elif kind == "rest":
+            start, size = block * rows + self.dup, rows - self.dup
         elif kind == "carried":
             start, size = block * rows + (p.par * h if h else 0), rows - h
         elif kind == "mine":
             start, size = block * rows + p.par * (rows - h), h
         else:
             start, size = block * rows + (1 - p.par) * (rows - h), h
-        return self.buf.at[pl.ds(pl.multiple_of(start, 16), size), :]
+        return self.buf.at[pl.ds(pl.multiple_of(start, 16), size), self.cols]
 
     def copy(self, ref, kind, sd, rd, dev):
+        kind += 6 * self.chunk
         return pltpu.make_async_remote_copy(
             src_ref=ref,
             dst_ref=ref,
@@ -71,8 +81,14 @@
             return self.copy(
                 self.part("carried", p.block(zs, 0)), 0, i, self.sem(d, s + 1), {"mp": nxt}
             )
+        if what == "dup":
+            nxt = p.me - 4 if d == 0 else p.me + 4
+            return self.copy(
+                self.part("dup", p.block(zs, 1)), 2, i, self.sem(d, s + 1), {"mp": nxt}
+            )
         if what == "y":
-            return self.copy(self.part("carried", p.block(zs, 0)), 1, i, i, p.ydev)
+            kind = "rest" if self.dup and s > 0 else "carried"
+            return self.copy(self.part(kind, p.block(zs, 0)), 1, i, i, p.ydev)
         kind, rel = what
         if kind == "x":
             return self.copy(self.part("mine", p.block(zs, rel)), 2 + rel, i, i, p.xdev)
@@ -84,8 +100,11 @@
         i = self.sem(d, s)
         if what == "z":
             self.copy(self.part("carried", p.block(zs, 0)), 0, i, i, p.ydev).wait_recv()
+        elif what == "dup":
+            self.copy(self.part("dup", p.block(zs, 1)), 2, i, i, p.ydev).wait_recv()
         elif what == "y":
-            self.copy(self.part("carried", p.block(zs, 1)), 1, i, i, p.ydev).wait_recv()
+            kind = "rest" if self.dup and s > 0 else "carried"
+            self.copy(self.part(kind, p.block(zs, 1)), 1, i, i, p.ydev).wait_recv()
         else:
             kind, rel = what
             if kind == "x":
@@ -107,9 +126,11 @@
         for d in (0, 1):
             pl.when(self.there(d, s))(functools.partial(f, d, s))
 
-    def begin(self):
+    def begin_z(self):
         for d in (0, 1):
             pl.when(self.onward(d))(lambda d=d: self.copies("z", d, 0).start())
+
+    def begin_plane(self):
         self.copies("y", 0, 0).start()
         self.copies(("c", 0), 0, 0).start()
 
@@ -128,10 +149,17 @@
 
     def y_step(self, s):
         def f(d, s):
+            if self.dup and s > 0:
+                self.arrived("dup", d, s)
+                if s < self.p.nz - 1:
+                    pl.when(self.onward(d))(lambda: self.copies("dup", d, s).start())
             self.arrived("y", d, s)
             self.copies(("x", 1) if self.share else ("c", 1), d, s).start()
 
         self.each(s, f)
+        if self.dup and s == 0:
+            for d in (0, 1):
+                pl.when(self.onward(d))(lambda d=d: self.copies("dup", d, 0).start())
 
     def x_step(self, s):
         if not self.share:
@@ -166,21 +194,25 @@
                     self.copies(("x", 1), d, s).wait_send()
                 if 0 < s < self.p.nz - 1:
                     pl.when(self.onward(d))(lambda: self.copies("z", d, s).wait_send())
+                    if self.dup:
+                        pl.when(self.onward(d))(lambda: self.copies("dup", d, s).wait_send())
 
             self.each(s, f)
         for d in (0, 1):
             pl.when(self.onward(d))(lambda d=d: self.copies("z", d, 0).wait_send())
-
-
-def tiles(width, f, size=512):
+            if self.dup:
+                pl.when(self.onward(d))(lambda d=d: self.copies("dup", d, 0).wait_send())
+
+
+def tiles(width, f, size=512, start=0):
     @pl.loop(0, width // size)
     def _(i):
-        f(pl.ds(pl.multiple_of(i * size, size), size))
+        f(pl.ds(pl.multiple_of(start + i * size, size), size))
 
 
 def kernel(
     n, groups, q_in, uo_in, ui_in, eig_in, tok_in, grad_in, out,
-    ui, uo, bt, tok, tin, acc, q, eig, m1t, xs, st,
+    ui, uo, bt, tok, tin, acc, parts, q, eig, m1t, xs, st,
     isend, irecv, osend, orecv, bsend, brecv, asend, arecv, local,
 ):
     p = Place(n, groups)
@@ -205,33 +237,37 @@
     pl.semaphore_signal(barrier, inc=1, device_id=p.xdev, device_id_type=MESH)
     pl.semaphore_wait(barrier, n)
 
-    gi = Gather(p, ui, rows, isend, irecv, True)
-    go = Gather(p, uo, rows, osend, orecv, True)
-    gb = Gather(p, bt, rows, bsend, brecv, False)
+    gi = [Gather(p, ui, rows, isend, irecv, True, h) for h in range(CHUNKS)]
+    go = [Gather(p, uo, rows, osend, orecv, True, h) for h in range(CHUNKS)]
+    gb = [Gather(p, bt, rows, bsend, brecv, False, h) for h in range(CHUNKS)]
 
     loads[0].wait()
-    gi.begin()
+    for g in gi:
+        g.begin_z()
+        g.begin_plane()
     for s in range(1, nz):
-        gi.z_step(s)
-        gi.y_step(s - 1)
+        for g in gi:
+            g.z_step(s)
+            g.y_step(s - 1)
         if s >= 2:
-            gi.x_step(s - 2)
-    gi.y_step(nz - 1)
+            for g in gi:
+                g.x_step(s - 2)
     loads[1].wait()
-    go.begin()
-    gi.x_step(nz - 2)
-    gi.x_step(nz - 1)
-    for s in range(nz):
-        gi.c_step(s)
+    for g in go:
+        g.begin_z()
+    for g in gi:
+        g.y_step(nz - 1)
+        g.x_step(nz - 2)
+    for g in go:
+        g.begin_plane()
+    for g in go:
+        g.z_step(1)
 
     loads[2].wait()
 
     def first(cols):
         m1 = jnp.dot(q[...], ui[:, cols], preferred_element_type=F32)
         m1t[cols, :] = m1.T.astype(BF)
-
-    tiles(width, first)
-    xs[pl.ds(me, 1)] = m1t[own, :][None]
 
     def exchange(k):
         to = lax.rem(me + k, n)
@@ -254,8 +290,15 @@
             device_id_type=MESH,
         )
 
-    for k in range(1, n):
-        exchange(k).start()
+    for g in gi:
+        g.x_step(nz - 1)
+        for s in range(nz):
+            g.c_step(s)
+        tiles(g.width, first, start=g.chunk * g.width)
+        for k in range(1, n):
+            now = lax.rem(me + k, n) // (n // CHUNKS) == g.chunk
+            pl.when(now)(lambda k=k: exchange(k).start())
+    xs[pl.ds(me, 1)] = m1t[own, :][None]
 
     loads[3].wait()
     piece = tokens // nz
@@ -269,19 +312,24 @@
         tiles(width, f)
 
     for s in range(1, nz):
-        go.z_step(s)
-        go.y_step(s - 1)
+        for g in go:
+            if s > 1:
+                g.z_step(s)
+            g.y_step(s - 1)
         if s >= 2:
-            go.x_step(s - 2)
+            for g in go:
+                g.x_step(s - 2)
         rotate_tokens(s - 1)
-    go.y_step(nz - 1)
-    go.x_step(nz - 2)
+    for g in go:
+        g.y_step(nz - 1)
+        g.x_step(nz - 2)
     rotate_tokens(nz - 1)
     grads = pltpu.make_async_copy(grad_in, tok, local.at[5])
     grads.start()
-    go.x_step(nz - 1)
-    for s in range(nz):
-        go.c_step(s)
+    for g in go:
+        g.x_step(nz - 1)
+        for s in range(nz):
+            g.c_step(s)
     for k in range(1, n):
         exchanged(k).wait_recv()
     loads[4].wait()
@@ -306,12 +354,14 @@
         )
         bt[own, cols] = b.astype(BF)
 
-    tiles(do, third)
-    gb.begin()
+    for g in gb:
+        tiles(g.width, third, start=g.chunk * g.width)
+        g.begin_z()
+        g.begin_plane()
 
     step = 384 if tokens % 384 == 0 else tokens
 
-    def add_plane(first, d, s):
+    def add_plane(g, first, d, s):
         zs = p.z + s if d == 0 else p.z - s
         k = pl.ds(pl.multiple_of(zs * 4 * rows, 4 * rows), 4 * rows)
 
@@ -320,44 +370,46 @@
             r = pl.ds(pl.multiple_of(t * step, step), step)
 
             def f(cols):
-                new = jnp.dot(tin_part(r, zs), bt[k, cols], preferred_element_type=F32)
+                new = jnp.dot(tin[r, k], bt[k, cols], preferred_element_type=F32)
                 if first:
                     acc[r, cols] = new
                 else:
                     acc[r, cols] += new
 
-            tiles(do, f)
-
-    def tin_part(r, zs):
-        if 4 * rows % 128 == 0:
-            return tin[r, pl.ds(pl.multiple_of(zs * 4 * rows, 4 * rows), 4 * rows)]
-        raise ValueError("rows")
+            tiles(g.width, f, start=g.chunk * g.width)
+
+    def add_scores(g):
+        @pl.loop(0, out.shape[0])
+        def _(t):
+            r = pl.ds(pl.multiple_of(t * 128, 128), 128)
+            part = jnp.zeros((128, 128), F32) if g.chunk == 0 else parts[r, :]
+            for j in range(g.width // 128):
+                cols = slice(g.chunk * g.width + j * 128, g.chunk * g.width + (j + 1) * 128)
+                part += tok[r, cols].astype(F32) * acc[r, cols]
+            if g.chunk == CHUNKS - 1:
+                out[pl.ds(t, 1), :] = jnp.sum(part.T, axis=0, keepdims=True)
+            else:
+                parts[r, :] = part
 
     for s in range(1, nz):
-        gb.z_step(s)
-        gb.y_step(s - 1)
-        gb.c_step(s - 1)
-        if s == 1:
-            add_plane(True, 0, 0)
-        else:
-            gb.each(s - 1, functools.partial(add_plane, False))
-    gb.y_step(nz - 1)
-    gb.c_step(nz - 1)
-    gb.each(nz - 1, functools.partial(add_plane, False))
-
+        for g in gb:
+            g.z_step(s)
+            g.y_step(s - 1)
+        for g in gb:
+            g.c_step(s - 1)
+            if s == 1:
+                add_plane(g, True, 0, 0)
+            else:
+                g.each(s - 1, functools.partial(add_plane, g, False))
+    for g in gb:
+        g.y_step(nz - 1)
     grads.wait()
-    step2 = out.shape[1]
-
-    @pl.loop(0, out.shape[0])
-    def _(t):
-        r = pl.ds(pl.multiple_of(t * step2, step2), step2)
-        part = jnp.zeros((step2, 128), F32)
-        for j in range(do // 128):
-            cols = slice(j * 128, (j + 1) * 128)
-            part += tok[r, cols].astype(F32) * acc[r, cols]
-        out[pl.ds(t, 1), :] = jnp.sum(part.T, axis=0, keepdims=True)
-
-    for g in (gi, go, gb):
+    for g in gb:
+        g.c_step(nz - 1)
+        g.each(nz - 1, functools.partial(add_plane, g, False))
+        add_scores(g)
+
+    for g in gi + go + gb:
         g.end()
     for k in range(1, n):
         exchange(k).wait_send()
@@ -384,13 +436,14 @@
                 pltpu.VMEM((tokens, di), BF),
                 pltpu.VMEM((tokens, di), BF),
                 pltpu.VMEM((tokens, do), F32),
+                pltpu.VMEM((tokens, 128), F32),
                 pltpu.VMEM((rows, di), BF),
                 pltpu.VMEM((do, eigen_vals.shape[1]), F32),
                 pltpu.VMEM((di, rows), BF),
                 pltpu.VMEM((n, rows, rows), BF),
                 pltpu.VMEM((rows, do), BF),
             ]
-            + [dma((6, 2 * nz))] * 6
+            + [dma((6 * CHUNKS, 2 * nz))] * 6
             + [dma((n,)), dma((n,)), dma((6,))],
             compiler_params=pltpu.CompilerParams(
                 collective_id=0, has_side_effects=True, vmem_limit_bytes=60 * 2**20

time: 165 us -> 152 us (0.921)
  Pallas kernels: 162 us -> 149 us
    pallas_call x1, Pallas kernels: 162 us -> 149 us  [shards(): pl.pallas_call(functools.partial(kernel, n, groups), out_shape=jax.ShapeD...]
where the time goes in v2:
time: 152 us; the launch traced here: 150 us
  Pallas kernels  149 us (98%)
    pallas_call x1, Pallas kernels, shards(): pl.pallas_call(functools.partial(kernel, n, groups), out_shape=jax.ShapeD...  149 us

profile of v2, /device:TPU:0, one launch (start us, length us, event | category | flops | bytes accessed | tf_op | source)
XLA Modules:
  0.0 150.0 jit_solution(13627361092961127044)
XLA Ops:
  0.0 148.7 %shard_map.64 = f32[12,128]{1,0:T(8,128)} custom-call(bf16[128,2048]{1,0:T(8,128)(2,1)} %q_in.1, bf16[128,2048]{1,0:T(8,128)(2,1)} %uo_in.1, bf16[128,2048]{1,0:T(8,128)(2,1)} %ui_in.1, f32[2048,128]{1,0:T(8,128)} %eig_in.1, bf16[1536,2048]{1,0:T(8,128)(2,1)} %tok_in.1, bf16[1536,2048]{1,0:T(8,128)(2,1)} %grad_in.1), custom_call_target="tpu_custom_call" | custom-call | tf_op jit(solution)/shard_map/pallas_call | solution.py:427
  148.7 1.3 copy.8
